TPU v7x, 32 devices: a whole 2x2x4 slice. The times are simulated.
32 devices in a mesh: section: 2 (over x), dp: 16 (over z, y, core).
Axes of the slice: x: 2, y: 2, z: 4, core: 2. Of those that a mesh axis runs over, the one named last changes fastest.
Arguments:
- inputs: bfloat16 [2, 32, 512, 512], P('section', 'dp'), may hold values from -6 to 6
- cotangent: bfloat16 [2, 32, 512, 512], P('section', 'dp'), may hold values from -6 to 6
- lengths: int32 [2, 32, 16], P(None, 'dp'), may hold values from 1 to 256, 512 in all within a row
- running: int32 [2, 32, 512], P('section', 'dp'), may hold values 0 or 1
- norm_gain: float32 [2, 2, 512], P('section'), may hold values from 0.25 to 1.75
- norm_shift: float32 [2, 2, 512], P('section'), may hold values from -1.5 to 1.5
- qkv_weight: bfloat16 [2, 512, 1536], P('section'), may hold values from -0.25 to 0.25
- out_weight: bfloat16 [2, 512, 512], P('section'), may hold values from -2 to 2
- up_weight: bfloat16 [2, 512, 2048], P('section'), may hold values from -0.25 to 0.25
- up_bias: float32 [2, 2048], P('section'), may hold values from -2.5 to 2.5
- down_weight: bfloat16 [2, 2048, 512], P('section'), may hold values from -0.125 to 0.125
- down_bias: float32 [2, 512], P('section'), may hold values from -2.5 to 2.5
- halt_weight: float32 [2, 512], P('section'), may hold values from -0.25 to 0.25
- halt_bias: float32 [2], P('section'), may hold values from -1 to 1
- cross_gain: float32 [512], replicated, may hold values from 0.25 to 1.75
- cross_shift: float32 [512], replicated, may hold values from -1.5 to 1.5
- cross_query: bfloat16 [512, 512], replicated, may hold values from -0.25 to 0.25
- cross_kv: bfloat16 [512, 1024], replicated, may hold values from -0.25 to 0.25
- cross_out: bfloat16 [512, 512], replicated, may hold values from -2 to 2
Outputs:
- activations: bfloat16 [2, 32, 512, 512], P('section', 'dp')
- input_grad: float32 [2, 32, 512, 512], P('section', 'dp')
- row_rms: float32 [2, 32, 2], P('section', 'dp')
- norm_gain_grad: float32 [2, 2, 512], P('section')
- norm_shift_grad: float32 [2, 2, 512], P('section')
- qkv_weight_grad: float32 [2, 512, 1536], P('section')
- out_weight_grad: float32 [2, 512, 512], P('section')
- up_weight_grad: float32 [2, 512, 2048], P('section')
- up_bias_grad: float32 [2, 2048], P('section')
- down_weight_grad: float32 [2, 2048, 512], P('section')
- down_bias_grad: float32 [2, 512], P('section')
- halt_weight_grad: float32 [2, 512], P('section')
- halt_bias_grad: float32 [2], P('section')
- cross_gain_grad: float32 [512], replicated
- cross_shift_grad: float32 [512], replicated
- cross_query_grad: float32 [512, 512], replicated
- cross_kv_grad: float32 [512, 1024], replicated
- cross_out_grad: float32 [512, 512], replicated
Inputs may be any that keep to these rules, and one draw needn't show every extreme that they name: Each row's 16 sentence lengths sum to 512; sentence k of a row's source pairs with sentence k of its target.
All inputs are finite; a program needn't handle non-finite values. No bound on the sum of `running` on one device may be relied on, other than what follows from the above.
Results may differ from a plain program's by a relative error of at most 0.025.
Values may be sent and summed in bfloat16 or wider, within the bound.
No kernel may reach another device: no remote copies, remote signals or barrier semaphores. Data moves between devices by JAX's collectives and lax.ppermute only.
A program may use at most 192 MiB of HBM per device.

v0:
```python
import jax
import jax.numpy as jnp
from jax import lax
from jax.sharding import PartitionSpec as P

HEADS = 8
L = 512
QB = 512


def from_behind(value, axis, steps):
    count = lax.axis_size(axis)
    initial, last = (max(0, -steps), min(count, count - steps))
    return lax.ppermute(value, axis, [(source, source + steps) for source in range(initial, last)])


def project(operand, weight):
    return jnp.einsum("rlk,kn->rln", operand, weight, preferred_element_type=jnp.float32)


def project_back(gradient, weight):
    return jnp.einsum("rln,kn->rlk", gradient, weight, preferred_element_type=jnp.float32)


def weight_grad(operand, gradient):
    return jnp.einsum("rlk,rln->kn", operand, gradient, preferred_element_type=jnp.float32)


def layer_norm(current, gain_vec, shift_vec):
    centered = current - jnp.mean(current, axis=-1, keepdims=True)
    spread = jnp.mean(centered * centered, axis=-1, keepdims=True)
    return centered * lax.rsqrt(spread + 1e-05) * gain_vec + shift_vec


def norm_back(current, gain_vec, shift_vec, gradient):
    outputs, pullback = jax.vjp(layer_norm, current, gain_vec, shift_vec)
    return pullback(gradient)


def gelu_tanh(pre_act):
    return jax.nn.gelu(pre_act, approximate=True)


def halting(current, updated, weight, offset, running_f):
    halt_rate = jax.nn.sigmoid(jnp.sum(current * weight, axis=-1) + offset)
    return current + (running_f * halt_rate)[..., None] * (updated - current)


def segment_ids(lengths):
    boundaries = jnp.cumsum(lengths, axis=-1, dtype=jnp.int32)
    places = jnp.arange(L, dtype=jnp.int32)
    return jnp.sum(
        (places[None, :, None] >= boundaries[:, None, :]).astype(jnp.int32),
        axis=-1,
        dtype=jnp.int32,
    )


def block_mask(query_seg, key_seg, start, causal):
    query_pos = start + jnp.arange(query_seg.shape[1], dtype=jnp.int32)
    key_pos = jnp.arange(key_seg.shape[1], dtype=jnp.int32)
    ordered = (key_pos[None, :] <= query_pos[:, None]) | (causal == 0)
    return ((query_seg[:, :, None] == key_seg[:, None, :]) & ordered[None])[:, None]


def split_heads(array_in):
    return array_in.reshape(array_in.shape[0], array_in.shape[1], HEADS, array_in.shape[2] // HEADS)


def attend_forward(queries, key_rows, values, query_seg, key_seg, causal):
    row_count, length, feature_count = queries.shape
    score_scale = (feature_count // HEADS) ** (-0.5)
    query_heads = split_heads(queries)
    key_heads = split_heads(key_rows)
    value_heads = split_heads(values)

    def one_block(block_index):
        start = block_index * QB
        allowed = block_mask(query_seg, key_seg, start, causal)
        scores = (
            jnp.einsum(
                "rqhd,rkhd->rhqk", query_heads, key_heads, preferred_element_type=jnp.float32
            )
            * score_scale
        )
        scores = jnp.where(allowed, scores, -1000000000.0)
        row_max = jnp.max(scores, axis=-1, keepdims=True)
        expanded = jnp.exp(scores - row_max)
        denominator = jnp.sum(expanded, axis=-1, keepdims=True)
        weights = (expanded / denominator).astype(jnp.bfloat16)
        attended = jnp.einsum(
            "rhqk,rkhd->rqhd", weights, value_heads, preferred_element_type=jnp.float32
        )
        return (attended.astype(jnp.bfloat16), (row_max + jnp.log(denominator))[..., 0])

    attended, log_total = lax.map(one_block, jnp.arange(length // QB, dtype=jnp.int32))
    attended = jnp.moveaxis(attended, 0, 1).reshape(row_count, length, feature_count)
    return (attended, log_total)


def attend_backward(queries, key_rows, values, log_total, grad_out, query_seg, key_seg, causal):
    row_count, length, feature_count = queries.shape
    score_scale = (feature_count // HEADS) ** (-0.5)
    query_heads = split_heads(queries)
    key_heads = split_heads(key_rows)
    value_heads = split_heads(values)
    grad_heads = split_heads(grad_out)

    def one_block(carry, block_index):
        key_grad, value_grad = carry
        start = block_index * QB
        log_block = lax.dynamic_index_in_dim(log_total, block_index, 0, keepdims=False)
        allowed = block_mask(query_seg, key_seg, start, causal)
        scores = (
            jnp.einsum(
                "rqhd,rkhd->rhqk", query_heads, key_heads, preferred_element_type=jnp.float32
            )
            * score_scale
        )
        scores = jnp.where(allowed, scores, -1000000000.0)
        probability = jnp.exp(scores - log_block[..., None])
        grad_weights = jnp.einsum(
            "rqhd,rkhd->rhqk", grad_heads, value_heads, preferred_element_type=jnp.float32
        )
        grad_scores = probability * (
            grad_weights - jnp.sum(grad_weights * probability, axis=-1, keepdims=True)
        )
        grad_scores = grad_scores.astype(jnp.bfloat16)
        query_grad = (
            jnp.einsum(
                "rhqk,rkhd->rqhd", grad_scores, key_heads, preferred_element_type=jnp.float32
            )
            * score_scale
        )
        key_grad = (
            key_grad
            + jnp.einsum(
                "rhqk,rqhd->rkhd", grad_scores, query_heads, preferred_element_type=jnp.float32
            )
            * score_scale
        )
        value_grad = value_grad + jnp.einsum(
            "rhqk,rqhd->rkhd",
            probability.astype(jnp.bfloat16),
            grad_heads,
            preferred_element_type=jnp.float32,
        )
        return ((key_grad, value_grad), query_grad.astype(jnp.bfloat16))

    zero_heads = jnp.zeros(key_heads.shape, jnp.float32)
    (key_grad, value_grad), query_grad = lax.scan(
        one_block, (zero_heads, zero_heads), jnp.arange(length // QB, dtype=jnp.int32)
    )
    query_grad = jnp.moveaxis(query_grad, 0, 1).reshape(row_count, length, feature_count)
    key_grad = key_grad.reshape(key_rows.shape).astype(jnp.bfloat16)
    value_grad = value_grad.reshape(values.shape).astype(jnp.bfloat16)
    return (query_grad, key_grad, value_grad)


def self_forward(current, gain_vec, shift_vec, w_qkv, w_out, segments, causal):
    feature_count = current.shape[-1]
    normed = layer_norm(current, gain_vec, shift_vec).astype(jnp.bfloat16)
    packed = project(normed, w_qkv).astype(jnp.bfloat16)
    queries = packed[..., :feature_count]
    key_rows = packed[..., feature_count : 2 * feature_count]
    values = packed[..., 2 * feature_count :]
    attended, log_total = attend_forward(queries, key_rows, values, segments, segments, causal)
    after_self = current + project(attended, w_out)
    return (after_self, (normed, queries, key_rows, values, attended, log_total))


def self_backward(current, grad_after, kept, gain_vec, shift_vec, w_qkv, w_out, segments, causal):
    normed, queries, key_rows, values, attended, log_total = kept
    grad_branch = grad_after.astype(jnp.bfloat16)
    out_grad = weight_grad(attended, grad_branch)
    grad_attended = project_back(grad_branch, w_out).astype(jnp.bfloat16)
    query_grad, key_grad, value_grad = attend_backward(
        queries, key_rows, values, log_total, grad_attended, segments, segments, causal
    )
    grad_packed = jnp.concatenate([query_grad, key_grad, value_grad], axis=-1)
    qkv_grad = weight_grad(normed, grad_packed)
    grad_in, gain_grad, shift_grad = norm_back(
        current, gain_vec, shift_vec, project_back(grad_packed, w_qkv)
    )
    return (grad_after + grad_in, gain_grad, shift_grad, qkv_grad, out_grad)


def feed_forward(current, ffn_params):
    gain_vec, shift_vec, w_up, up_offset, w_down, down_offset = ffn_params
    normed = layer_norm(current, gain_vec, shift_vec).astype(jnp.bfloat16)
    pre_act = project(normed, w_up) + up_offset
    activated = gelu_tanh(pre_act).astype(jnp.bfloat16)
    return (current + project(activated, w_down) + down_offset, (normed, pre_act, activated))


def feed_backward(current, grad_after, kept, ffn_params):
    gain_vec, shift_vec, w_up, up_offset, w_down, down_offset = ffn_params
    normed, pre_act, activated = kept
    grad_branch = grad_after.astype(jnp.bfloat16)
    down_grad = weight_grad(activated, grad_branch)
    down_offset_grad = jnp.sum(grad_branch.astype(jnp.float32), axis=(0, 1))
    grad_act = project_back(grad_branch, w_down)
    outputs, pullback = jax.vjp(gelu_tanh, pre_act)
    grad_pre = pullback(grad_act)[0].astype(jnp.bfloat16)
    up_grad = weight_grad(normed, grad_pre)
    up_offset_grad = jnp.sum(grad_pre.astype(jnp.float32), axis=(0, 1))
    grad_in, gain_grad, shift_grad = norm_back(
        current, gain_vec, shift_vec, project_back(grad_pre, w_up)
    )
    return (
        grad_after + grad_in,
        (gain_grad, shift_grad, up_grad, up_offset_grad, down_grad, down_offset_grad),
    )


def shards(
    inputs,
    cotangent,
    lengths,
    running,
    norm_gain,
    norm_shift,
    qkv_weight,
    out_weight,
    up_weight,
    up_bias,
    down_weight,
    down_bias,
    halt_weight,
    halt_bias,
    cross_gain,
    cross_shift,
    cross_query,
    cross_kv,
    cross_out,
):
    section_index = lax.axis_index("section")
    decoding = section_index == 1
    current = inputs[0].astype(jnp.float32)
    running_f = running[0].astype(jnp.float32)
    src_seg = segment_ids(lengths[0])
    tgt_seg = segment_ids(lengths[1])
    own_seg = jnp.where(decoding, tgt_seg, src_seg)
    feature_count = current.shape[-1]
    ffn_params = (
        norm_gain[0, 1],
        norm_shift[0, 1],
        up_weight[0],
        up_bias[0],
        down_weight[0],
        down_bias[0],
    )
    halt_vec = halt_weight[0]
    halt_offset = halt_bias[0]

    def halt_local(state_in, updated_in, vec_in, offset_in):
        return halting(state_in, updated_in, vec_in, offset_in, running_f)

    after_self, self_kept = self_forward(
        current,
        norm_gain[0, 0],
        norm_shift[0, 0],
        qkv_weight[0],
        out_weight[0],
        own_seg,
        section_index,
    )

    def encoder_head(after):
        updated, unused = feed_forward(after, ffn_params)
        return halt_local(current, updated, halt_vec, halt_offset)

    def decoder_head(after):
        return after

    first_out = lax.cond(decoding, decoder_head, encoder_head, after_self)
    memory_low = first_out.astype(jnp.bfloat16)
    received = from_behind(memory_low, "section", 1)

    def decoder_tail(operands):
        after, arrived = operands
        normed_c = layer_norm(after, cross_gain, cross_shift).astype(jnp.bfloat16)
        cross_queries = project(normed_c, cross_query).astype(jnp.bfloat16)
        cross_pairs = project(arrived, cross_kv).astype(jnp.bfloat16)
        cross_keys = cross_pairs[..., :feature_count]
        cross_values = cross_pairs[..., feature_count:]
        cross_att, cross_log = attend_forward(
            cross_queries, cross_keys, cross_values, tgt_seg, src_seg, 0
        )
        after_cross = after + project(cross_att, cross_out)
        updated, ffn_kept = feed_forward(after_cross, ffn_params)
        result, pullback = jax.vjp(halt_local, current, updated, halt_vec, halt_offset)
        grad_current, grad_updated, vec_grad, offset_grad = pullback(
            cotangent[0].astype(jnp.float32)
        )
        grad_cross, ffn_grads = feed_backward(after_cross, grad_updated, ffn_kept, ffn_params)
        grad_branch = grad_cross.astype(jnp.bfloat16)
        cross_out_grad = weight_grad(cross_att, grad_branch)
        grad_att = project_back(grad_branch, cross_out).astype(jnp.bfloat16)
        query_grad, key_grad, value_grad = attend_backward(
            cross_queries, cross_keys, cross_values, cross_log, grad_att, tgt_seg, src_seg, 0
        )
        cross_query_grad = weight_grad(normed_c, query_grad)
        grad_in, cross_gain_grad, cross_shift_grad = norm_back(
            after, cross_gain, cross_shift, project_back(query_grad, cross_query)
        )
        grad_pairs = jnp.concatenate([key_grad, value_grad], axis=-1)
        tail_grads = ffn_grads + (vec_grad, offset_grad)
        cross_grads = (
            cross_gain_grad,
            cross_shift_grad,
            cross_query_grad,
            jnp.zeros(cross_kv.shape, jnp.float32),
            cross_out_grad,
        )
        return (result, grad_cross + grad_in, grad_current, grad_pairs, tail_grads, cross_grads)

    def encoder_rest(operands):
        after, arrived = operands
        zero_rows = jnp.zeros(after.shape, jnp.float32)
        zero_vec = jnp.zeros((feature_count,), jnp.float32)
        returned_zero = jnp.zeros(after.shape[:-1] + (2 * feature_count,), jnp.bfloat16)
        tail_zero = (
            zero_vec,
            zero_vec,
            jnp.zeros(up_weight[0].shape, jnp.float32),
            jnp.zeros(up_bias[0].shape, jnp.float32),
            jnp.zeros(down_weight[0].shape, jnp.float32),
            jnp.zeros(down_bias[0].shape, jnp.float32),
            zero_vec,
            jnp.zeros((), jnp.float32),
        )
        cross_zero = (
            zero_vec,
            zero_vec,
            jnp.zeros(cross_query.shape, jnp.float32),
            jnp.zeros(cross_kv.shape, jnp.float32),
            jnp.zeros(cross_out.shape, jnp.float32),
        )
        return (zero_rows, zero_rows, zero_rows, returned_zero, tail_zero, cross_zero)

    tail_out = lax.cond(decoding, decoder_tail, encoder_rest, (after_self, received))
    result, dec_grad_after, dec_grad_halt, returned_grad, dec_tail_grads, cross_grads = tail_out
    returned = from_behind(returned_grad, "section", -1)

    def encoder_tail():
        updated, ffn_kept = feed_forward(after_self, ffn_params)
        kv_extra = weight_grad(memory_low, returned)
        grad_memory = lax.optimization_barrier(
            project_back(returned, cross_kv).astype(jnp.bfloat16)
        ).astype(jnp.float32)
        grad_result = cotangent[0].astype(jnp.float32) + grad_memory
        outputs, pullback = jax.vjp(halt_local, current, updated, halt_vec, halt_offset)
        grad_current, grad_updated, vec_grad, offset_grad = pullback(grad_result)
        grad_after, ffn_grads = feed_backward(after_self, grad_updated, ffn_kept, ffn_params)
        return (grad_after, grad_current, ffn_grads + (vec_grad, offset_grad), kv_extra)

    def decoder_keep():
        return (
            dec_grad_after,
            dec_grad_halt,
            dec_tail_grads,
            jnp.zeros(cross_kv.shape, jnp.float32),
        )

    grad_after, grad_halt, tail_grads, kv_extra = lax.cond(decoding, decoder_keep, encoder_tail)
    grad_input, gain_grad, shift_grad, qkv_grad, out_grad = self_backward(
        current,
        grad_after,
        self_kept,
        norm_gain[0, 0],
        norm_shift[0, 0],
        qkv_weight[0],
        out_weight[0],
        own_seg,
        section_index,
    )
    input_grad = grad_input + grad_halt
    final = jnp.where(decoding, result, first_out)
    change = final - current
    row_rms = jnp.stack(
        [
            jnp.sqrt(jnp.mean(final * final, axis=(1, 2)) + 1e-06),
            jnp.sqrt(jnp.mean(change * change, axis=(1, 2)) + 1e-06),
        ],
        axis=-1,
    )
    summed = lax.psum(
        (
            jnp.stack([gain_grad, tail_grads[0]])[None],
            jnp.stack([shift_grad, tail_grads[1]])[None],
            qkv_grad[None],
            out_grad[None],
            tail_grads[2][None],
            tail_grads[3][None],
            tail_grads[4][None],
            tail_grads[5][None],
            tail_grads[6][None],
            jnp.reshape(tail_grads[7], (1,)),
        ),
        "dp",
    )
    crossed = lax.psum(
        (cross_grads[0], cross_grads[1], cross_grads[2], cross_grads[3] + kv_extra, cross_grads[4]),
        ("section", "dp"),
    )
    return (
        final.astype(jnp.bfloat16)[None],
        input_grad[None],
        row_rms[None],
        summed[0],
        summed[1],
        summed[2],
        summed[3],
        summed[4],
        summed[5],
        summed[6],
        summed[7],
        summed[8],
        summed[9],
        crossed[0],
        crossed[1],
        crossed[2],
        crossed[3],
        crossed[4],
    )


def solution(mesh):
    in_specs = (
        P("section", "dp", None, None),
        P("section", "dp", None, None),
        P(None, "dp", None),
        P("section", "dp", None),
        P("section", None, None),
        P("section", None, None),
        P("section", None, None),
        P("section", None, None),
        P("section", None, None),
        P("section", None),
        P("section", None, None),
        P("section", None),
        P("section", None),
        P("section"),
        P(),
        P(),
        P(),
        P(),
        P(),
    )
    out_specs = (
        P("section", "dp", None, None),
        P("section", "dp", None, None),
        P("section", "dp", None),
        P("section", None, None),
        P("section", None, None),
        P("section", None, None),
        P("section", None, None),
        P("section", None, None),
        P("section", None),
        P("section", None, None),
        P("section", None),
        P("section", None),
        P("section"),
        P(),
        P(),
        P(),
        P(),
        P(),
    )
    return jax.shard_map(shards, mesh=mesh, in_specs=in_specs, out_specs=out_specs, check_vma=False)
```

profile of v0, /device:TPU:0, one launch (start us, length us, event | category | flops | bytes accessed | tf_op | source)
XLA Modules:
  0.0 792.8 jit_solution(12260590158612893547)
XLA Ops:
  28.4 10.0 %fusion.161 = (f32[2,8,512]{2,1,0:T(8,128)S(1)}, f32[2,8,512,512]{2,3,1,0:T(8,128)}) fusion(bf16[2,512,8,64]{1,3,2,0:T(8,128)(2,1)} %bitcast.298, bf16[2,512,8,64]{1,3,2,0:T(8,128)(2,1)} %bitcast.292, pred[2,512,512]{1,2,0:T(8,128)(4,1)S(1)} %compare_and_fusion), kind=kOutput, calls=%fused_computation.260 | convolution fusion | flops 549445632 | bytes 19431424 | tf_op jit(solution)/shard_map/while/body/eval_jaxpr/rqhd,rkhd->rhqk/dot_general | solution.py:81
  38.5 8.4 %fusion.109 = f32[2,8,512]{2,1,0:T(8,128)S(1)} fusion(f32[2,8,512,512]{2,3,1,0:T(8,128)} %get-tuple-element.816, f32[2,8,512]{2,1,0:T(8,128)S(1)} %get-tuple-element.815), kind=kLoop, calls=%fused_computation.173 | loop fusion | flops 8380416 | bytes 16842752 | tf_op jit(solution)/shard_map/while/body/eval_jaxpr/reduce_sum | solution.py:89
  46.9 7.6 fusion.122
  56.6 16.0 %conditional.7 = (f32[2,512,512]{2,1,0:T(8,128)}) conditional(s32[]{:T(128)} %convert_element_type.244, (f32[1,512]{1,0:T(1,128)S(1)}, f32[2,512,512]{2,1,0:T(8,128)}, f32[]{:T(128)}, f32[2,512]{1,0:T(2,128)S(1)}, f32[2,512,512]{2,1,0:T(8,128)}, /*index=5*/f32[1,1,512]{2,1,0:T(1,128)S(1)}, f32[1,1,512]{2,1,0:T(1,128)S(1)}, ...), branch_computations={%region_8.12_spmd, %region_12.13_spmd} | conditional | flops 4324332544 | bytes 16850960
  61.9 10.3 %multiply_add_fusion = f32[2,512,512]{2,1,0:T(8,128)} fusion(f32[2,512,512]{2,1,0:T(8,128)} %get-tuple-element.409, f32[2,512,512]{2,1,0:T(8,128)} %get-tuple-element.413, bf16[2048,512]{0,1:T(8,128)(2,1)} %get-tuple-element.639, f32[2048]{0:T(1024)S(1)} %bitcast.364, bf16[512,2048]{1,0:T(8,128)(2,1)} %get-tuple-element.416, f32[512]{0:T(512)S(1)} %bitcast.371, ...), kind=kOutput, calls=%fused_computation.13 | convolution fusion | flops 4321181696 | bytes 10512384 | tf_op jit(solution)/shard_map/cond/branch_0_fun/rlk,kn->rln/dot_general | solution.py:18
  77.6 22.6 %collective-permute-done = bf16[2,512,512]{1,2,0:T(8,128)(2,1)} collective-permute-done((bf16[2,512,512]{1,2,0:T(8,128)(2,1)}, bf16[2,512,512]{1,2,0:T(8,128)(2,1)}, u32[]{:S(2)}, u32[]{:S(2)}) %collective-permute-start) | collective-permute-done | bytes 1048608 | tf_op jit(solution)/shard_map/ppermute | solution.py:14
  100.2 20.6 %conditional.8 = (f32[2,512,512]{1,2,0:T(8,128)}, f32[2,512,512]{1,2,0:T(8,128)}, bf16[2,512,1024]{1,2,0:T(8,128)(2,1)}, f32[512]{0:T(512)S(1)}, f32[512]{0:T(51...) conditional(s32[]{:T(128)} %convert_element_type.244, () %tuple.81, ...), branch_computations={%region_13.14_spmd, %region_14.36_spmd} | conditional | flops 20624971776 | bytes 564913088 | solution.py:342
  120.9 4.1 copy.191
  126.3 185.4 %collective-permute-done.1 = bf16[2,512,1024]{2,1,0:T(8,128)(2,1)S(1)} collective-permute-done((bf16[2,512,1024]{2,1,0:T(8,128)(2,1)}, bf16[2,512,1024]{2,1,0:T(8,128)(2,1)S(1)}, u32[]{:S(2)}, u32[]{:S(2)}) %collective-permute-start.1) | collective-permute-done | bytes 2097184 | tf_op jit(solution)/shard_map/ppermute | solution.py:14
  311.7 41.1 %conditional.10 = (f32[2,512,512]{2,1,0:T(8,128)S(1)}, f32[2,512,512]{2,1,0:T(8,128)S(1)}, f32[512,2048]{1,0:T(8,128)}, f32[2048]{0:T(1024)S(1)}, f32[2048,512]{...) conditional(s32[]{:T(128)} %convert_element_type.244, ...), branch_computations={%region_36.49_spmd.clone, %region_49.50_spmd.clone} | conditional | flops 15156654080 | bytes 174272832
  323.9 4.1 multiply_reduce_fusion.13
  329.7 8.1 %convert_reduce_fusion.2 = (f32[2048]{0:T(1024)S(1)}, bf16[2,512,2048]{2,1,0:T(8,128)(2,1)S(1)}) fusion(f32[2,512,2048]{2,1,0:T(8,128)S(1)} %fusion.92, f32[2048]{0:T(1024)S(1)} %bitcast.369, bf16[2,512,512]{2,1,0:T(8,128)(2,1)S(1)} %get-tuple-element.772, bf16[2048,512]{0,1:T(8,128)(2,1)S(1)} %copy-done.44), kind=kOutput, calls=%fused_computation.128 | convolution fusion | flops 2195716096 | bytes 15745024 | tf_op jit(solution)/shard_map/cond/branch_0_fun/rln,kn->rlk/dot_general | solution.py:22
  337.9 4.5 convolution_bitcast_fusion.4
  345.0 4.6 convolution_bitcast_fusion.5
  356.1 4.0 broadcast_add_fusion
  360.1 11.1 %multiply_reduce_fusion.17 = (f32[2,8,512]{2,1,0:T(8,128)S(1)}, f32[2,8,512,512]{2,3,1,0:T(8,128)}) fusion(f32[2,8,512,512]{2,3,1,0:T(8,128)} %get-tuple-element.816, f32[2,8,512]{2,1,0:T(8,128)S(1)} %log_add_fusion.1, bf16[2,512,8,64]{1,3,2,0:T(8,128)(2,1)S(1)} %bitcast.296, bf16[2,512,8,64]{1,3,2,0:T(8,128)(2,1)S(1)} %bitcast.309), kind=kOutput, calls=%fused_computation.168 | convolution fusion | flops 549445632 | bytes 35717120 | tf_op jit(solution)/shard_map/while/body/eval_jaxpr/rqhd,rkhd->rhqk/dot_general | solution.py:122
  371.3 15.2 %multiply_convert_fusion.9 = bf16[2,8,512,512]{2,3,1,0:T(8,128)(2,1)} fusion(f32[2,8,512,512]{2,3,1,0:T(8,128)} %get-tuple-element.818, f32[2,8,512,512]{2,3,1,0:T(8,128)} %get-tuple-element.816, f32[2,8,512]{2,1,0:T(8,128)S(1)} %get-tuple-element.817, f32[2,8,512]{2,1,0:T(8,128)S(1)} %log_add_fusion.1), kind=kLoop, calls=%fused_computation.167 | loop fusion | flops 16777216 | bytes 42008576 | tf_op jit(solution)/shard_map/while/body/eval_jaxpr/convert_element_type | solution.py:128
  386.7 9.4 %fusion.123 = bf16[2,8,64,512]{3,2,1,0:T(8,128)(2,1)} fusion(bf16[2,512,8,64]{1,3,2,0:T(8,128)(2,1)S(1)} %bitcast.297, f32[2,8,512,512]{2,3,1,0:T(8,128)} %get-tuple-element.816, f32[2,8,512]{2,1,0:T(8,128)S(1)} %log_add_fusion.1), kind=kOutput, calls=%fused_computation.205 | convolution fusion | flops 545783808 | bytes 18907136 | tf_op jit(solution)/shard_map/while/body/eval_jaxpr/rhqk,rqhd->rkhd/dot_general | solution.py:142
  398.5 5.9 multiply_convert_fusion.11
  406.8 7.1 multiply_convert_fusion.10
  423.8 39.9 %all-reduce = (f32[512]{0:T(512)}, f32[512]{0:T(512)}) all-reduce(f32[512]{0:T(512)S(1)} %get-tuple-element.533, f32[512]{0:T(512)S(1)} %get-tuple-element.534), channel_id=1, replica_groups=mesh['section'=2,'dp'=16] {'section','dp'}, use_global_device_ids=true, to_apply=%region_67.68 | all-reduce | flops 1024 | bytes 8192 | tf_op jit(solution)/shard_map/psum | solution.py:403
  470.8 61.1 %all-reduce.2 = (f32[1,2,512]{2,1,0:T(2,128)}, f32[1,2,512]{2,1,0:T(2,128)}, f32[1,2048]{1,0:T(1,128)}, f32[1,512]{1,0:T(1,128)}, f32[1,512]{1,0:T(1,128)}, /*index=5*/f32[1]{0:T(128)}) all-reduce(f32[1,2,512]{2,1,0:T(2,128)S(1)} %maximum_bitcast_fusion, ...), channel_id=1, replica_groups=mesh['section'=2,'dp'=16] {'dp'}, use_global_device_ids=true, to_apply=%region_56.57 | all-reduce | flops 5121 | bytes 40968 | tf_op jit(solution)/shard_map/psum | solution.py:388
  531.9 4.2 add_bitcast_fusion
  536.1 234.2 %all-reduce.9.cloned.1.call-done = (f32[1,512,1536]{2,1,0:T(8,128)}, f32[1,512,512]{2,1,0:T(8,128)}, f32[1,512,2048]{2,1,0:T(8,128)}, f32[1,2048,512]{2,1,0:T(8,128)}) async-done(((f32[1,512,1536]{2,1,0:T(8,128)}, f32[1,512,512]{2,1,0:T(8,128)}, f32[1,512,2048]{2,1,0:T(8,128)}, f32[1,2048,512]{2,1,0:T(8,128)}), (f32[1,512,1536]{2,1,0:T(8,128)}, f32[1,512,512]{2,1,0:T(8,128)}, f32[1,512,2048]{2,1,0:T(8,128)}, ...) | async-done | bytes 12582928 | tf_op jit(solution)/shard_map/psum | solution.py:388
  (203 shorter events, 108.1 us)
Async XLA Ops:
  7.2 10.2 %copy-start = (bf16[1,512,1536]{2,1,0:T(8,128)(2,1)S(1)}, bf16[1,512,1536]{2,1,0:T(8,128)(2,1)}, u32[]{:S(2)}) copy-start(bf16[1,512,1536]{2,1,0:T(8,128)(2,1)} %param.31) | copy-start | bytes 4718596
  7.2 528.9 %all-reduce.7.cloned.1.call-start = ((), (), s32[]{:S(2)}) async-start(), calls=%async_computation | async-start | bytes 8388608 | tf_op jit(solution)/shard_map/psum | solution.py:403
  12.1 5.2 copy-start.62
  38.5 8.4 %copy-start.58 = (f32[2,8,512]{2,1,0:T(8,128)}, f32[2,8,512]{2,1,0:T(8,128)S(1)}, u32[]{:S(2)}) copy-start(f32[2,8,512]{2,1,0:T(8,128)S(1)} %get-tuple-element.815) | copy-start | bytes 98308
  38.5 8.4 %copy-start.30 = (bf16[2,512,512]{1,2,0:T(8,128)(2,1)S(1)}, bf16[2,512,512]{1,2,0:T(8,128)(2,1)}, u32[]{:S(2)}) copy-start(bf16[2,512,512]{1,2,0:T(8,128)(2,1)} %copy.177) | copy-start | bytes 3145732
  46.9 7.6 copy-start.60
  46.9 7.6 copy-start.40
  72.6 27.6 %copy-start.19 = (bf16[1,2,512,512]{3,2,1,0:T(8,128)(2,1)S(1)}, bf16[1,2,512,512]{3,2,1,0:T(8,128)(2,1)}, u32[]{:S(2)}) copy-start(bf16[1,2,512,512]{3,2,1,0:T(8,128)(2,1)} %param.26) | copy-start | bytes 3145732
  72.7 27.6 %copy-start.69 = (f32[512]{0:T(512)S(1)}, f32[512]{0:T(512)}, u32[]{:S(2)}) copy-start(f32[512]{0:T(512)} %param.39) | copy-start | bytes 6148
  72.7 27.6 %copy-start.85 = (f32[512]{0:T(512)S(1)}, f32[512]{0:T(512)}, u32[]{:S(2)}) copy-start(f32[512]{0:T(512)} %param.40) | copy-start | bytes 6148
  75.3 24.9 %collective-permute-start = (bf16[2,512,512]{1,2,0:T(8,128)(2,1)}, bf16[2,512,512]{1,2,0:T(8,128)(2,1)}, u32[]{:S(2)}, u32[]{:S(2)}) collective-permute-start(bf16[2,512,512]{1,2,0:T(8,128)(2,1)} %copy.184), channel_id=1, source_target_pairs={{0,16},{1,17},{2,18},{3,19},{4,20},{5,21},{6,22},{7,23},{8,24},{9,... | collective-permute-start | bytes 3145736 | tf_op jit(solution)/shard_map/ppermute | solution.py:14
  120.8 5.4 copy-start.59
  120.9 5.4 copy-start.61
  120.9 190.8 %copy-start.20 = (bf16[1,2,512,512]{3,2,1,0:T(8,128)(2,1)S(1)}, bf16[1,2,512,512]{3,2,1,0:T(8,128)(2,1)}, u32[]{:S(2)}) copy-start(bf16[1,2,512,512]{3,2,1,0:T(8,128)(2,1)} %param.26) | copy-start | bytes 3145732
  124.9 186.7 %collective-permute-start.1 = (bf16[2,512,1024]{2,1,0:T(8,128)(2,1)}, bf16[2,512,1024]{2,1,0:T(8,128)(2,1)S(1)}, u32[]{:S(2)}, u32[]{:S(2)}) collective-permute-start(bf16[2,512,1024]{2,1,0:T(8,128)(2,1)} %copy.191), channel_id=1, source_target_pairs={{16,0},{17,1},{18,2},{19,3},{20,4},{21,5},{22,6},{23,7},{24,8},{25... | collective-permute-start | bytes 6291464 | tf_op jit(solution)/shard_map/ppermute | solution.py:14
  311.7 43.1 %copy-start.41 = (bf16[1,512,512]{2,1,0:T(8,128)(2,1)S(1)}, bf16[1,512,512]{2,1,0:T(8,128)(2,1)}, u32[]{:S(2)}) copy-start(bf16[1,512,512]{2,1,0:T(8,128)(2,1)} %param.32) | copy-start | bytes 1572868
  354.7 5.4 copy-start.12
  354.8 5.4 copy-start.26
  386.5 383.8 %all-reduce.9.cloned.1.call-start = ((), (), s32[]{:S(2)}) async-start(), calls=%async_computation.1 | async-start | bytes 25165824 | tf_op jit(solution)/shard_map/psum | solution.py:388
  406.8 13.2 %copy-start.63 = (f32[2,512]{1,0:T(2,128)S(1)}, f32[2,512]{1,0:T(2,128)}, u32[]{:S(2)}) copy-start(f32[2,512]{1,0:T(2,128)} %copy-done.62) | copy-start | bytes 12292
  406.8 13.2 %copy-start.66 = (f32[2,512]{1,0:T(2,128)S(1)}, f32[2,512]{1,0:T(2,128)}, u32[]{:S(2)}) copy-start(f32[2,512]{1,0:T(2,128)} %copy-done.65) | copy-start | bytes 12292
  406.8 13.2 %copy-start.71 = (f32[1,1,512]{2,1,0:T(1,128)S(1)}, f32[1,1,512]{2,1,0:T(1,128)}, u32[]{:S(2)}) copy-start(f32[1,1,512]{2,1,0:T(1,128)} %copy-done.70) | copy-start | bytes 6148
  406.8 13.2 %copy-start.77 = (f32[1,1,512]{2,1,0:T(1,128)S(1)}, f32[1,1,512]{2,1,0:T(1,128)}, u32[]{:S(2)}) copy-start(f32[1,1,512]{2,1,0:T(1,128)} %copy-done.76) | copy-start | bytes 6148
  770.3 4.9 copy-start.37
  (38 other events, 108.1 us)
Sparse Core Ops, SparseCore 0:
  386.6 143.8 all-reduce.6
  536.7 233.4 all-reduce.8
where the time goes:
time: 803 us; the launch traced here: 793 us
  waiting for transfers between devices  442 us (55%)
  matrix products  106 us (13%)
  blocking collectives  101 us (13%)
  local copies, waits for them, and re-layouts  61.6 us (8%)
  other arithmetic  54.8 us (7%)
  between operations  14.8 us (2%)
  loops' own time  8.15 us (1%)
    psum x1, waiting for transfers between devices, shards(): lax.psum((jnp.stack([gain_grad, tail_grads[0]])[None], jnp.stack([shift_g...  234 us
    ppermute x2, waiting for transfers between devices, from_behind(): lax.ppermute(value, axis, [(source, source + steps) for source in range(i...  208 us
    psum x1, blocking collectives, shards(): lax.psum((jnp.stack([gain_grad, tail_grads[0]])[None], jnp.stack([shift_g...  61.1 us
    psum x1, blocking collectives, shards(): lax.psum((cross_grads[0], cross_grads[1], cross_grads[2], cross_grads[3]...  39.9 us
    unnamed x124, local copies, waits for them, and re-layouts  25.2 us
    dot_general x5, matrix products, project(): jnp.einsum('rlk,kn->rln', operand, weight, preferred_element_type=jnp.flo...  20.8 us
    dot_general x5, matrix products, weight_grad(): jnp.einsum('rlk,rln->kn', operand, gradient, preferred_element_type=jnp.f...  17.8 us
    dot_general x5, matrix products, project_back(): jnp.einsum('rln,kn->rlk', gradient, weight, preferred_element_type=jnp.fl...  16.6 us
  transfers between devices with their start and end apart: 4, of which 3 were waited for; matrix products, arithmetic and copies ran while one was open for 6% of the time, Pallas kernels for 0%

commit v1 on v0

--- a/solution.py
+++ b/solution.py
@@ -211,6 +211,24 @@
         grad_after + grad_in,
         (gain_grad, shift_grad, up_grad, up_offset_grad, down_grad, down_offset_grad),
     )
+
+
+def gather_sums(own, crossing, width):
+    count = lax.axis_size("dp")
+
+    def laid_out(arrays):
+        return jnp.concatenate(
+            [array.astype(jnp.bfloat16).reshape(count, -1, width) for array in arrays], axis=1
+        )
+
+    held = jnp.concatenate([laid_out(own), laid_out(crossing)], axis=1)
+    own_rows = sum(array.size for array in own) // (width * count)
+    share = lax.psum_scatter(held.reshape(-1, width), "dp", tiled=True)
+    cross_share = share[own_rows:]
+    swapped = lax.ppermute(cross_share, "section", [(0, 1), (1, 0)])
+    cross_share = cross_share.astype(jnp.float32) + swapped.astype(jnp.float32)
+    share = jnp.concatenate([share[:own_rows], cross_share.astype(jnp.bfloat16)])
+    return lax.all_gather(share, "dp")
 
 
 def shards(
@@ -385,44 +403,48 @@
         ],
         axis=-1,
     )
-    summed = lax.psum(
-        (
-            jnp.stack([gain_grad, tail_grads[0]])[None],
-            jnp.stack([shift_grad, tail_grads[1]])[None],
-            qkv_grad[None],
-            out_grad[None],
-            tail_grads[2][None],
-            tail_grads[3][None],
-            tail_grads[4][None],
-            tail_grads[5][None],
-            tail_grads[6][None],
-            jnp.reshape(tail_grads[7], (1,)),
-        ),
-        "dp",
-    )
-    crossed = lax.psum(
-        (cross_grads[0], cross_grads[1], cross_grads[2], cross_grads[3] + kv_extra, cross_grads[4]),
-        ("section", "dp"),
-    )
+    vectors = jnp.concatenate(
+        [
+            jnp.stack([gain_grad, tail_grads[0], shift_grad, tail_grads[1]]),
+            tail_grads[3].reshape(-1, feature_count),
+            jnp.stack([tail_grads[5], tail_grads[6]]),
+            jnp.full((1, feature_count), tail_grads[7]),
+            jnp.stack([cross_grads[0], cross_grads[1]]),
+        ]
+    )
+    vectors = jnp.sum(lax.all_gather(vectors, "dp"), axis=0)
+    cross_vectors = vectors[-2:] + lax.ppermute(vectors[-2:], "section", [(0, 1), (1, 0)])
+    count = lax.axis_size("dp")
+    own = (qkv_grad, out_grad, tail_grads[2], tail_grads[4])
+    crossing = (cross_grads[2], cross_grads[3] + kv_extra, cross_grads[4])
+    own_rows = [array.size // (feature_count * count) for array in own]
+    cross_rows = [array.size // (feature_count * count) for array in crossing]
+    gathered = gather_sums(own, crossing, feature_count)
+    summed, place = [], 0
+    for array, rows in zip(own + crossing, own_rows + cross_rows):
+        summed.append(
+            gathered[:, place : place + rows].reshape(array.shape).astype(jnp.float32)
+        )
+        place += rows
     return (
         final.astype(jnp.bfloat16)[None],
         input_grad[None],
         row_rms[None],
-        summed[0],
-        summed[1],
-        summed[2],
-        summed[3],
+        vectors[None, 0:2],
+        vectors[None, 2:4],
+        summed[0][None],
+        summed[1][None],
+        summed[2][None],
+        vectors[4:-5].reshape(1, -1),
+        summed[3][None],
+        vectors[None, -5],
+        vectors[None, -4],
+        vectors[-3, :1],
+        cross_vectors[0],
+        cross_vectors[1],
         summed[4],
         summed[5],
         summed[6],
-        summed[7],
-        summed[8],
-        summed[9],
-        crossed[0],
-        crossed[1],
-        crossed[2],
-        crossed[3],
-        crossed[4],
     )
 
 

time: 803 us -> 686 us (0.85)
  waiting for transfers between devices: 442 us -> 354 us
  blocking collectives: 101 us -> 24.8 us
  local copies, waits for them, and re-layouts: 61.6 us -> 85 us
  other arithmetic: 54.8 us -> 74.2 us
    psum x2 -> x0, waiting for transfers between devices: 234 us -> none  [the longest x1 234 us: shards(): lax.psum((jnp.stack([gain_grad, tail_grads[0]])[None], jnp.stack([shift_g...]
    reduce_scatter x0 -> x1, waiting for transfers between devices: none -> 105 us  [gather_sums(): share = lax.psum_scatter(held.reshape(-1, width), 'dp', tiled=True)]
    psum x2 -> x0, blocking collectives: 101 us -> none  [the longest x1 61.1 us: shards(): lax.psum((jnp.stack([gain_grad, tail_grads[0]])[None], jnp.stack([shift_g...]
    all_gather x0 -> x1, waiting for transfers between devices: none -> 33.8 us  [gather_sums(): return lax.all_gather(share, 'dp')]
    all_gather x0 -> x1, blocking collectives: none -> 24.8 us  [shards(): vectors = jnp.sum(lax.all_gather(vectors, 'dp'), axis=0)]
    convert_element_type x0 -> x9, other arithmetic: none -> 19.8 us  [the longest x6 14.2 us: shards(): gathered[:, place:place + rows].reshape(array.shape).astype(jnp.float32)]
    convert_element_type x0 -> x3, local copies, waits for them, and re-layouts: none -> 13.4 us  [shards(): gathered[:, place:place + rows].reshape(array.shape).astype(jnp.float32)]
    reshape x0 -> x6, local copies, waits for them, and re-layouts: none -> 12 us  [the longest x5 12 us: laid_out(): array.astype(jnp.bfloat16).reshape(count, -1, width)]
  transfers between devices with their start and end apart: 4 -> 6, of which waited for: 3 -> 5; matrix products, arithmetic and copies ran while one was open for 6% -> 2% of each run, Pallas kernels for 0% -> 0%
where the time goes in v1:
time: 686 us; the launch traced here: 675 us
  waiting for transfers between devices  354 us (52%)
  matrix products  108 us (16%)
  local copies, waits for them, and re-layouts  85 us (12%)
  other arithmetic  74.2 us (11%)
  blocking collectives  24.8 us (4%)
  between operations  14.9 us (2%)
  starting transfers between devices  8.46 us (1%)
    ppermute x2, waiting for transfers between devices, from_behind(): lax.ppermute(value, axis, [(source, source + steps) for source in range(i...  212 us
    reduce_scatter x1, waiting for transfers between devices, gather_sums(): share = lax.psum_scatter(held.reshape(-1, width), 'dp', tiled=True)  105 us
    all_gather x1, waiting for transfers between devices, gather_sums(): return lax.all_gather(share, 'dp')  33.8 us
    all_gather x1, blocking collectives, shards(): vectors = jnp.sum(lax.all_gather(vectors, 'dp'), axis=0)  24.8 us
    dot_general x5, matrix products, weight_grad(): jnp.einsum('rlk,rln->kn', operand, gradient, preferred_element_type=jnp.f...  22.5 us
    dot_general x5, matrix products, project_back(): jnp.einsum('rln,kn->rlk', gradient, weight, preferred_element_type=jnp.fl...  21 us
    dot_general x5, matrix products, project(): jnp.einsum('rlk,kn->rln', operand, weight, preferred_element_type=jnp.flo...  21 us
    unnamed x91, local copies, waits for them, and re-layouts  18 us
  transfers between devices with their start and end apart: 6, of which 5 were waited for; matrix products, arithmetic and copies ran while one was open for 2% of the time, Pallas kernels for 0%

profile of v1, /device:TPU:0, one launch (start us, length us, event | category | flops | bytes accessed | tf_op | source)
XLA Modules:
  0.0 674.9 jit_solution(17604471928116772958)
XLA Ops:
  28.4 10.0 %fusion.168 = (f32[2,8,512]{2,1,0:T(8,128)S(1)}, f32[2,8,512,512]{2,3,1,0:T(8,128)}) fusion(bf16[2,512,8,64]{1,3,2,0:T(8,128)(2,1)} %bitcast.317, bf16[2,512,8,64]{1,3,2,0:T(8,128)(2,1)} %bitcast.313, pred[2,512,512]{1,2,0:T(8,128)(4,1)S(1)} %compare_and_fusion), kind=kOutput, calls=%fused_computation.285 | convolution fusion | flops 549445632 | bytes 19431424 | tf_op jit(solution)/shard_map/while/body/eval_jaxpr/rqhd,rkhd->rhqk/dot_general | solution.py:81
  38.5 8.4 %fusion.111 = f32[2,8,512]{2,1,0:T(8,128)S(1)} fusion(f32[2,8,512,512]{2,3,1,0:T(8,128)} %get-tuple-element.801, f32[2,8,512]{2,1,0:T(8,128)S(1)} %get-tuple-element.800), kind=kLoop, calls=%fused_computation.175 | loop fusion | flops 8380416 | bytes 16842752 | tf_op jit(solution)/shard_map/while/body/eval_jaxpr/reduce_sum | solution.py:89
  46.9 7.6 %fusion.125 = bf16[2,8,64,512]{3,2,1,0:T(8,128)(2,1)S(1)} fusion(bf16[2,512,8,64]{1,3,2,0:T(8,128)(2,1)S(1)} %bitcast.333, f32[2,8,512,512]{2,3,1,0:T(8,128)} %get-tuple-element.801, f32[2,8,512]{2,1,0:T(8,128)S(1)} %fusion.111, f32[2,8,512]{2,1,0:T(8,128)S(1)} %get-tuple-element.800), kind=kOutput, calls=%fused_computation.210 | convolution fusion | flops 549978112 | bytes 18939904 | tf_op jit(solution)/shard_map/while/body/eval_jaxpr/rhqk,rkhd->rqhd/dot_general | solution.py:91
  56.6 15.9 %conditional.7 = (f32[2,512,512]{2,1,0:T(8,128)}) conditional(s32[]{:T(128)} %convert_element_type.349, (f32[1,512]{1,0:T(1,128)S(1)}, f32[2,512,512]{2,1,0:T(8,128)}, f32[]{:T(128)}, f32[2,512]{1,0:T(2,128)S(1)}, f32[2,512,512]{2,1,0:T(8,128)}, /*index=5*/f32[1,1,512]{2,1,0:T(1,128)S(1)}, f32[1,1,512]{2,1,0:T(1,128)S(1)}, ...), branch_computations={%region_8.12_spmd, %region_12.13_spmd} | conditional | flops 4324332544 | bytes 16850960
  61.9 10.3 %multiply_add_fusion = f32[2,512,512]{2,1,0:T(8,128)} fusion(f32[2,512,512]{2,1,0:T(8,128)} %get-tuple-element.416, f32[2,512,512]{2,1,0:T(8,128)} %get-tuple-element.420, bf16[2048,512]{0,1:T(8,128)(2,1)} %get-tuple-element.687, f32[2048]{0:T(1024)S(1)} %bitcast.398, bf16[512,2048]{1,0:T(8,128)(2,1)} %get-tuple-element.423, f32[512]{0:T(512)S(1)} %bitcast.405, ...), kind=kOutput, calls=%fused_computation.13 | convolution fusion | flops 4321181696 | bytes 10512384 | tf_op jit(solution)/shard_map/cond/branch_0_fun/rlk,kn->rln/dot_general | solution.py:18
  77.5 22.6 %collective-permute-done = bf16[2,512,512]{1,2,0:T(8,128)(2,1)} collective-permute-done((bf16[2,512,512]{1,2,0:T(8,128)(2,1)}, bf16[2,512,512]{1,2,0:T(8,128)(2,1)}, u32[]{:S(2)}, u32[]{:S(2)}) %collective-permute-start) | collective-permute-done | bytes 1048608 | tf_op jit(solution)/shard_map/ppermute | solution.py:14
  100.2 15.4 %conditional.8 = (f32[2,512,512]{1,2,0:T(8,128)}, f32[2,512,512]{1,2,0:T(8,128)}, bf16[2,512,1024]{1,2,0:T(8,128)(2,1)}, f32[512]{0:T(512)S(1)}, f32[512]{0:T(51...) conditional(s32[]{:T(128)} %convert_element_type.349, () %tuple.95, ...), branch_computations={%region_13.14_spmd, %region_14.36_spmd} | conditional | flops 20625496064 | bytes 559670208 | solution.py:360
  121.0 189.4 %collective-permute-done.1 = bf16[2,512,1024]{2,1,0:T(8,128)(2,1)S(1)} collective-permute-done((bf16[2,512,1024]{2,1,0:T(8,128)(2,1)}, bf16[2,512,1024]{2,1,0:T(8,128)(2,1)S(1)}, u32[]{:S(2)}, u32[]{:S(2)}) %collective-permute-start.1) | collective-permute-done | bytes 2097184 | tf_op jit(solution)/shard_map/ppermute | solution.py:14
  310.4 58.3 %conditional.9 = (f32[2,512,512]{2,1,0:T(8,128)S(1)}, f32[2,512,512]{2,1,0:T(8,128)}, bf16[2048,512]{1,0:T(8,128)(2,1)}, f32[]{:T(128)}, f32[512,1024]{1,0:T(8,1...) conditional(s32[]{:T(128)} %convert_element_type.349, ...), branch_computations={%region_36.49_spmd, %region_49.50_spmd} | conditional | flops 15158224896 | bytes 225673696
  326.0 4.3 multiply_reduce_fusion.13
  332.1 5.1 convolution_bitcast_fusion.4
  337.2 8.8 %convert_reduce_fusion.2 = (f32[2048]{0:T(1024)S(1)}, bf16[2,512,2048]{2,1,0:T(8,128)(2,1)}) fusion(f32[2,512,2048]{2,1,0:T(8,128)S(1)} %fusion.94, f32[2048]{0:T(1024)S(1)} %bitcast.404, bf16[2,512,512]{2,1,0:T(8,128)(2,1)S(1)} %get-tuple-element.746, bf16[2048,512]{0,1:T(8,128)(2,1)S(1)} %copy-done.42), kind=kOutput, calls=%fused_computation.130 | convolution fusion | flops 2195716096 | bytes 15745024 | tf_op jit(solution)/shard_map/cond/branch_0_fun/rln,kn->rlk/dot_general | solution.py:22
  346.1 6.9 %bitcast_convert_fusion = bf16[512,2048]{1,0:T(8,128)(2,1)} fusion(bf16[2,512,2048]{2,1,0:T(8,128)(2,1)} %get-tuple-element.777, f32[2,512,512]{2,1,0:T(8,128)} %get-tuple-element.455, f32[512]{0:T(512)S(1)} %bitcast.392, f32[512]{0:T(512)S(1)} %bitcast.358, f32[2,512]{1,0:T(2,128)S(1)} %fusion.109, f32[2,512]{1,0:T(2,128)S(1)} %broadcast_multiply_fusion.3), kind=kOutput, calls=%fused_computation.132 | convolution fusion | flops 2151153664 | bytes 8400896 | tf_op jit(solution)/shard_map/cond/branch_0_fun/rlk,rln->kn/dot_general | solution.py:26
  356.8 4.4 reshape.509
  373.7 8.6 %fusion.126 = bf16[2,8,64,512]{3,2,1,0:T(8,128)(2,1)S(1)} fusion(bf16[2,512,8,64]{1,3,2,0:T(8,128)(2,1)S(1)} %bitcast.331, f32[2,8,512,512]{2,3,1,0:T(8,128)} %get-tuple-element.801, f32[2,8,512]{2,1,0:T(8,128)S(1)} %log_add_fusion.1), kind=kOutput, calls=%fused_computation.212 | convolution fusion | flops 545783808 | bytes 18907136 | tf_op jit(solution)/shard_map/while/body/eval_jaxpr/rhqk,rqhd->rkhd/dot_general | solution.py:142
  382.3 11.3 %multiply_reduce_fusion.17 = (f32[2,8,512]{2,1,0:T(8,128)S(1)}, f32[2,8,512,512]{2,3,1,0:T(8,128)}) fusion(f32[2,8,512,512]{2,3,1,0:T(8,128)} %get-tuple-element.801, f32[2,8,512]{2,1,0:T(8,128)S(1)} %log_add_fusion.1, bf16[2,512,8,64]{1,3,2,0:T(8,128)(2,1)S(1)} %bitcast.332, bf16[2,512,8,64]{1,3,2,0:T(8,128)(2,1)S(1)} %bitcast.334), kind=kOutput, calls=%fused_computation.170 | convolution fusion | flops 549445632 | bytes 35717120 | tf_op jit(solution)/shard_map/while/body/eval_jaxpr/rqhd,rkhd->rhqk/dot_general | solution.py:122
  393.6 11.8 %multiply_convert_fusion.9 = bf16[2,8,512,512]{2,3,1,0:T(8,128)(2,1)S(1)} fusion(f32[2,8,512,512]{2,3,1,0:T(8,128)} %get-tuple-element.803, f32[2,8,512,512]{2,3,1,0:T(8,128)} %get-tuple-element.801, f32[2,8,512]{2,1,0:T(8,128)S(1)} %get-tuple-element.802, f32[2,8,512]{2,1,0:T(8,128)S(1)} %log_add_fusion.1), kind=kLoop, calls=%fused_computation.169 | loop fusion | flops 16777216 | bytes 42008576 | tf_op jit(solution)/shard_map/while/body/eval_jaxpr/convert_element_type | solution.py:128
  420.9 5.0 fusion.117
  444.2 105.2 %reduce-scatter.2.cloned.1.call-done = bf16[512,512]{1,0:T(8,128)(2,1)} async-done(((bf16[8192,512]{1,0:T(8,128)(2,1)}), bf16[512,512]{1,0:T(8,128)(2,1)}) %reduce-scatter.2.cloned.1.call-update) | async-done | bytes 524304 | tf_op jit(solution)/shard_map/reduce_scatter | solution.py:226
  564.7 24.8 %all-gather.2 = f32[16,13,512]{2,1,0:T(8,128)S(1)} all-gather(f32[1,13,512]{2,1,0:T(8,128)S(1)} %bitcast.351), channel_id=2, replica_groups=mesh['section'=2,'dp'=16] {'dp'}, dimensions={0}, use_global_device_ids=true | all-gather | bytes 452608 | tf_op jit(solution)/shard_map/all_gather | solution.py:415
  593.4 5.0 add_bitcast_fusion
  601.4 33.8 %all-gather.5.cloned.1.call-done = bf16[8192,512]{1,0:T(8,128)(2,1)} async-done(((bf16[512,512]{1,0:T(8,128)(2,1)}), bf16[8192,512]{1,0:T(8,128)(2,1)}) %all-gather.5.cloned.1.call-update) | async-done | bytes 8388624 | tf_op jit(solution)/shard_map/all_gather | solution.py:231
  653.1 4.9 reshape.472
  662.2 5.6 reshape.474
  (226 shorter events, 160.8 us)
Async XLA Ops:
  7.2 10.2 %copy-start = (bf16[1,512,1536]{2,1,0:T(8,128)(2,1)S(1)}, bf16[1,512,1536]{2,1,0:T(8,128)(2,1)}, u32[]{:S(2)}) copy-start(bf16[1,512,1536]{2,1,0:T(8,128)(2,1)} %param.31) | copy-start | bytes 4718596
  7.2 542.2 %reduce-scatter.2.cloned.1.call-start = ((), (), s32[]{:S(2)}) async-start(), calls=%async_computation.1 | async-start | bytes 8912896 | tf_op jit(solution)/shard_map/reduce_scatter | solution.py:226
  38.5 8.4 %copy-start.52 = (f32[2,8,512]{2,1,0:T(8,128)}, f32[2,8,512]{2,1,0:T(8,128)S(1)}, u32[]{:S(2)}) copy-start(f32[2,8,512]{2,1,0:T(8,128)S(1)} %get-tuple-element.800) | copy-start | bytes 98308
  38.5 8.4 %copy-start.31 = (bf16[2,512,512]{1,2,0:T(8,128)(2,1)S(1)}, bf16[2,512,512]{1,2,0:T(8,128)(2,1)}, u32[]{:S(2)}) copy-start(bf16[2,512,512]{1,2,0:T(8,128)(2,1)} %copy.229) | copy-start | bytes 3145732
  46.9 7.6 %copy-start.54 = (f32[2,8,512]{2,1,0:T(8,128)}, f32[2,8,512]{2,1,0:T(8,128)S(1)}, u32[]{:S(2)}) copy-start(f32[2,8,512]{2,1,0:T(8,128)S(1)} %fusion.111) | copy-start | bytes 98308
  46.9 7.6 %copy-start.50 = (bf16[1,512,512]{2,1,0:T(8,128)(2,1)S(1)}, bf16[1,512,512]{2,1,0:T(8,128)(2,1)}, u32[]{:S(2)}) copy-start(bf16[1,512,512]{2,1,0:T(8,128)(2,1)} %param.32) | copy-start | bytes 1572868
  72.6 27.6 %copy-start.21 = (bf16[1,2,512,512]{3,2,1,0:T(8,128)(2,1)S(1)}, bf16[1,2,512,512]{3,2,1,0:T(8,128)(2,1)}, u32[]{:S(2)}) copy-start(bf16[1,2,512,512]{3,2,1,0:T(8,128)(2,1)} %param.26) | copy-start | bytes 3145732
  72.6 27.6 %copy-start.63 = (f32[512]{0:T(512)S(1)}, f32[512]{0:T(512)}, u32[]{:S(2)}) copy-start(f32[512]{0:T(512)} %param.39) | copy-start | bytes 6148
  72.6 27.6 %copy-start.79 = (f32[512]{0:T(512)S(1)}, f32[512]{0:T(512)}, u32[]{:S(2)}) copy-start(f32[512]{0:T(512)} %param.40) | copy-start | bytes 6148
  75.2 24.9 %collective-permute-start = (bf16[2,512,512]{1,2,0:T(8,128)(2,1)}, bf16[2,512,512]{1,2,0:T(8,128)(2,1)}, u32[]{:S(2)}, u32[]{:S(2)}) collective-permute-start(bf16[2,512,512]{1,2,0:T(8,128)(2,1)} %copy.236), channel_id=1, source_target_pairs={{0,16},{1,17},{2,18},{3,19},{4,20},{5,21},{6,22},{7,23},{8,24},{9,... | collective-permute-start | bytes 3145736 | tf_op jit(solution)/shard_map/ppermute | solution.py:14
  115.5 5.4 copy-start.53
  115.5 5.4 copy-start.55
  115.6 194.8 %copy-start.22 = (bf16[1,2,512,512]{3,2,1,0:T(8,128)(2,1)S(1)}, bf16[1,2,512,512]{3,2,1,0:T(8,128)(2,1)}, u32[]{:S(2)}) copy-start(bf16[1,2,512,512]{3,2,1,0:T(8,128)(2,1)} %param.26) | copy-start | bytes 3145732
  119.6 190.7 %collective-permute-start.1 = (bf16[2,512,1024]{2,1,0:T(8,128)(2,1)}, bf16[2,512,1024]{2,1,0:T(8,128)(2,1)S(1)}, u32[]{:S(2)}, u32[]{:S(2)}) collective-permute-start(bf16[2,512,1024]{2,1,0:T(8,128)(2,1)} %copy.243), channel_id=1, source_target_pairs={{16,0},{17,1},{18,2},{19,3},{20,4},{21,5},{22,6},{23,7},{24,8},{25... | collective-permute-start | bytes 6291464 | tf_op jit(solution)/shard_map/ppermute | solution.py:14
  320.1 11.4 %copy-start.37 = (bf16[2,512,512]{2,1,0:T(8,128)(2,1)}, bf16[2,512,512]{2,1,0:T(8,128)(2,1)S(1)}, u32[]{:S(2)}) copy-start(bf16[2,512,512]{2,1,0:T(8,128)(2,1)S(1)} %convolution_convert_fusion.3) | copy-start | bytes 3145732 | tf_op jit(solution)/shard_map/conditional.3
  346.0 6.9 %copy-start.2 = (f32[2,512,512]{2,1,0:T(8,128)S(1)}, f32[2,512,512]{2,1,0:T(8,128)}, u32[]{:S(2)}) copy-start(f32[2,512,512]{2,1,0:T(8,128)} %get-tuple-element.455) | copy-start | bytes 6291460 | tf_op jit(solution)/shard_map/conditional.3
  346.0 6.9 %copy-start.74 = (bf16[512,2048]{1,0:T(8,128)(2,1)S(1)}, bf16[512,2048]{1,0:T(8,128)(2,1)}, u32[]{:S(2)}) copy-start(bf16[512,2048]{1,0:T(8,128)(2,1)} %get-tuple-element.458) | copy-start | bytes 6291460 | tf_op jit(solution)/shard_map/conditional.3
  346.0 6.9 %copy-start.81 = (bf16[2,512,2048]{2,1,0:T(8,128)(2,1)S(1)}, bf16[2,512,2048]{2,1,0:T(8,128)(2,1)}, u32[]{:S(2)}) copy-start(bf16[2,512,2048]{2,1,0:T(8,128)(2,1)} %get-tuple-element.777) | copy-start | bytes 12582916 | tf_op jit(solution)/shard_map/conditional.3
  373.7 8.6 %copy-start.32 = (bf16[2,512,512]{1,2,0:T(8,128)(2,1)S(1)}, bf16[2,512,512]{1,2,0:T(8,128)(2,1)}, u32[]{:S(2)}) copy-start(bf16[2,512,512]{1,2,0:T(8,128)(2,1)} %copy.229) | copy-start | bytes 3145732
  393.6 11.8 %copy-start.20 = (bf16[2,512,512]{1,2,0:T(8,128)(2,1)S(1)}, bf16[2,512,512]{1,2,0:T(8,128)(2,1)}, u32[]{:S(2)}) copy-start(bf16[2,512,512]{1,2,0:T(8,128)(2,1)} %copy.230) | copy-start | bytes 3145732
  444.1 191.1 %all-gather.5.cloned.1.call-start = ((), (), s32[]{:S(2)}) async-start(), calls=%async_computation.2 | async-start | bytes 8912896 | tf_op jit(solution)/shard_map/all_gather | solution.py:231
  550.3 5.4 collective-permute-start.2
  589.5 10.7 %collective-permute-start.3 = (f32[2,512]{1,0:T(2,128)S(1)}, f32[2,512]{1,0:T(2,128)S(1)}, u32[]{:S(2)}, u32[]{:S(2)}) collective-permute-start(f32[2,512]{1,0:T(2,128)S(1)} %slice.133), channel_id=1, source_target_pairs={{0,16},{16,0},{1,17},{17,1},{2,18},{18,2},{3,19},{19,3},{4,20},{20... | collective-permute-start | bytes 12296 | tf_op jit(solution)/shard_map/ppermute | solution.py:416
  635.2 8.2 %copy-start.23 = (bf16[8192,512]{1,0:T(8,128)(2,1)S(1)}, bf16[8192,512]{1,0:T(8,128)(2,1)}, u32[]{:S(2)}) copy-start(bf16[8192,512]{1,0:T(8,128)(2,1)} %all-gather.5.cloned.1.call-done) | copy-start | bytes 25165828
  (36 other events, 120.5 us)
Sparse Core Ops, SparseCore 0:
  444.2 105.1 reduce-scatter.1
  557.6 77.5 all-gather.4
